TPU v7x, 32 devices: a whole 2x2x4 slice. The times are simulated.
32 devices in a mesh: orb: 8 (over z, core), dom: 4 (over y, x).
Axes of the slice: x: 2, y: 2, z: 4, core: 2. Of those that a mesh axis runs over, the one named last changes fastest.
Arguments:
- orbitals: bfloat16 [8, 16, 48, 128], P('orb', None, 'dom'), may hold values from -6 to 6
- potential: float32 [16, 48, 128], P(None, 'dom'), may hold values from 0 to 2
- degree: int32 [8], P('orb'), may hold values from 1 to 8, as said below
- owners: int32 [4], replicated, may hold values from 0 to 7
- rotation: bfloat16 [4, 1, 8], P(None, None, 'orb'), may hold values from -3 to 3
Outputs:
- filtered: float32 [8, 16, 48, 128], P('orb', None, 'dom')
- rotated: float32 [8, 16, 48, 128], P('orb', None, 'dom')
Inputs may be any that keep to these rules, and one draw needn't show every extreme that they name: Every draw has an orbital of degree 8 and one of degree 1. `owners`: panel numbers; panel q holds orbital q alone.
All inputs are finite; a program needn't handle non-finite values.
Results may differ from a plain program's by a relative error of at most 0.0003.
Values sent between devices are 32-bit elements; how exact they have to be, the bound alone decides.
No kernel may reach another device: no remote copies, remote signals or barrier semaphores. Data moves between devices by JAX's collectives and lax.ppermute only.
A program may use at most 64 MiB of HBM per device.

v0:
```python
import functools

import jax
import jax.numpy as jnp
import ml_dtypes
import numpy as np
from jax import lax
from jax.experimental import pallas as pl
from jax.experimental.pallas import tpu as pltpu
from jax.sharding import PartitionSpec as P

RADIUS = 6
MAXDEG = 8
STEPS = 4

STENCIL = (
    -5369.0 / 1800.0,
    12.0 / 7.0,
    -15.0 / 56.0,
    10.0 / 189.0,
    -1.0 / 112.0,
    2.0 / 1925.0,
    -1.0 / 16632.0,
)
FILTER_CENTER = 7.75
FILTER_HALF = 6.25
SCALE = 2.0 / FILTER_HALF
TAPS = tuple(-0.5 * SCALE * c for c in STENCIL[1:])
DIAGONAL = SCALE * (-1.5 * STENCIL[0] - FILTER_CENTER)


def xor_pairs(count, mask):
    return [(i, i ^ mask) for i in range(count)]


def shift_pairs(count, step):
    return [(i, i - step) for i in range(count) if 0 <= i - step < count]


def split(values):
    high = values.astype(jnp.bfloat16)
    return high, (values - high.astype(jnp.float32)).astype(jnp.bfloat16)


def stencil(count, cells):
    around = np.zeros((count, count), np.float64)
    for k, tap in enumerate(TAPS, 1):
        for i in range(count):
            around[i, (i + k) % count] += tap
            around[i, (i - k) % count] += tap
    between = sum(tap * (np.eye(cells, k=k) + np.eye(cells, k=-k)) for k, tap in enumerate(TAPS, 1))
    matrix = np.kron(np.eye(cells), around) + np.kron(between, np.eye(count))
    high = matrix.astype(ml_dtypes.bfloat16)
    low = (matrix - high.astype(np.float64)).astype(ml_dtypes.bfloat16)
    return high, low


class Layout:
    def __init__(self, n_dom, cells, planes, width):
        self.n_dom, self.cells, self.planes, self.width = n_dom, cells, planes, width
        halo = -(-RADIUS * MAXDEG // cells)
        self.whole = n_dom <= 2 * halo + 1
        if self.whole:
            self.slots = list(range(1, n_dom))
            self.pairs = [xor_pairs(n_dom, k) for k in self.slots]
            self.window = n_dom * cells
            extents = {min(cells + 2 * RADIUS * left, self.window) for left in range(MAXDEG)}
        else:
            self.slots = [s * k for k in range(1, halo + 1) for s in (1, -1)]
            self.pairs = [shift_pairs(n_dom, k) for k in self.slots]
            self.window = (2 * halo + 1) * cells
            extents = {cells}
        self.groups = sorted({max(g for g in range(1, width // planes + 1) if e % (2 * g) == 0) for e in extents})
        high, low = stencil(width, 1)
        across = np.block([[high, low], [high, low]])
        self.matrices = [across] + [np.block([[m, m] for m in stencil(planes, g)]) for g in self.groups]

    def home(self):
        return lax.axis_index("dom") if self.whole else self.window // self.cells // 2

    def starts(self):
        home = self.home()
        return [(home ^ k if self.whole else home + k) * self.cells for k in [0] + self.slots]

    def on_grid(self, reach, act):
        home, dom = self.home(), lax.axis_index("dom")
        for block in range(home - reach, home + reach + 1):
            place = dom + block - home
            pl.when((place >= 0) & (place < self.n_dom))(functools.partial(act, block))


def apply_taps(layout, matrices, source, target, shift, base, extent, begin):
    planes, width = layout.planes, layout.width
    high, low = split(source[pl.ds(RADIUS + base, extent)].reshape(extent * planes, width))
    across = jnp.dot(jnp.concatenate([high, low], 1), matrices[0][...], preferred_element_type=jnp.float32)
    group = max(m for m in layout.groups if extent % (2 * m) == 0)
    size = group * planes
    alongs = []
    for top in range(0, extent * planes, 2 * size):
        pieces = [jnp.concatenate([v[top : top + size], v[top + size : top + 2 * size]], 1) for v in (high, low)]
        matrix = matrices[1 + layout.groups.index(group)]
        alongs.append(jnp.dot(matrix[...], jnp.concatenate(pieces, 0), preferred_element_type=jnp.float32))
    for tile in range(0, extent, group):
        x = RADIUS + base + tile
        below = [source[x - RADIUS + j] for j in range(RADIUS)]
        above = [source[x + group + j] for j in range(RADIUS)]
        for i in range(group):
            terms = begin(base + tile + i)
            for k in range(1, RADIUS + 1):
                outside = ([below[RADIUS + i - k]] if i < k else []) + ([above[i + k - group]] if i + k >= group else [])
                if outside:
                    terms.append(TAPS[k - 1] * functools.reduce(jnp.add, outside))
            target[shift + base + tile + i] = functools.reduce(jnp.add, terms)
    for index, along in enumerate(alongs):
        along = along[:size] + along[size:]
        for half in range(2):
            top = (2 * index + half) * size
            plane_sum = across[top : top + size, :width] + across[top : top + size, width:]
            plane_sum = plane_sum + along[:, half * width : (half + 1) * width]
            spot = pl.ds(shift + base + (2 * index + half) * group, group)
            target[spot] = target[spot] + plane_sum.reshape(group, planes, width)


def halves_kernel(cells, coefficients_ref, *refs):
    *blocks, out_ref = refs
    half = cells // 2
    for index, block in enumerate(blocks):
        out_ref[pl.ds(index * half, half)] = block[cells:]
    out_ref[pl.ds(len(blocks) * half, 1)] = coefficients_ref[...]


def open_kernel(layout, *refs):
    count = len(layout.matrices)
    matrices, blocks, (start_ref, taps_ref) = refs[:count], refs[count:-2], refs[-2:]
    cells, window = layout.cells, layout.window
    edge = jnp.zeros((RADIUS, layout.planes, layout.width), jnp.float32)
    start_ref[pl.ds(0, RADIUS)] = edge
    start_ref[pl.ds(RADIUS + window, RADIUS)] = edge
    for start, block in zip(layout.starts(), blocks):
        start_ref[pl.ds(RADIUS + start, cells)] = block[:cells]

    def act(base, extent):
        apply_taps(layout, matrices, start_ref, taps_ref, 0, base, extent, lambda x: [])

    if layout.whole:
        act(0, window)
    else:
        taps_ref[...] = jnp.zeros(taps_ref.shape, jnp.float32)
        layout.on_grid(window // cells // 2, lambda block: act(block * cells, cells))


def chain_kernel(layout, degree_ref, *refs):
    count = len(layout.matrices)
    matrices, (own_ref, swapped_ref, start_ref, taps_ref), refs = refs[:count], refs[count : count + 4], refs[count + 4 :]
    blocks, (out_ref, *fields, potential) = refs[: len(layout.slots)], refs[len(layout.slots) :]
    cells, window = layout.cells, layout.window
    half = cells // 2
    core = lax.axis_index("orb") % 2
    degree = degree_ref[0]
    home = layout.home()

    starts = layout.starts()
    potential[pl.ds(starts[0], cells)] = SCALE * own_ref[...] + DIAGONAL
    for index, (start, block) in enumerate(zip(starts[1:], blocks)):
        potential[pl.ds(start + core * half, half)] = SCALE * block[cells:] + DIAGONAL
        other = swapped_ref[index * half : (index + 1) * half]
        potential[pl.ds(start + (1 - core) * half, half)] = SCALE * other + DIAGONAL

    def begin(current, previous):
        previous[...] = start_ref[...]
        current[pl.ds(0, RADIUS)] = start_ref[pl.ds(0, RADIUS)]
        current[pl.ds(RADIUS + window, RADIUS)] = start_ref[pl.ds(RADIUS + window, RADIUS)]
        for x in range(0, window, RADIUS):
            here = pl.ds(RADIUS + x, RADIUS)
            current[here] = 0.5 * (taps_ref[pl.ds(x, RADIUS)] + potential[pl.ds(x, RADIUS)] * start_ref[here])

    pl.when(degree % 2 == 1)(functools.partial(begin, fields[0], fields[1]))
    pl.when(degree % 2 == 0)(functools.partial(begin, fields[1], fields[0]))

    def level(parity, reach):
        source, target = fields[1 - parity], fields[parity]

        def act(base, extent):
            def first(x):
                return [potential[x] * source[RADIUS + x] - target[RADIUS + x]]

            apply_taps(layout, matrices, source, target, RADIUS, base, extent, first)

        if layout.whole:
            extent = min(cells + 2 * reach, window)
            act(jnp.clip(home * cells - reach, 0, window - extent), extent)
        else:
            layout.on_grid(-(-reach // cells), lambda block: act(block * cells, cells))

    def levels(fewest, most, reach):
        parity = fewest % 2
        total = jnp.maximum(jnp.minimum(most, degree - 2) - fewest + 1, 0)

        def pair(index, carry):
            level(1 - parity, reach)
            level(parity, reach)
            return carry

        pl.when(total % 2 == 1)(lambda: level(parity, reach))
        if most > fewest:
            lax.fori_loop(0, total // 2, pair, 0)

    bounds = [RADIUS * left for left in range(MAXDEG - 1)]
    if layout.whole:
        bounds = [min(reach, (window - cells + 1) // 2) for reach in bounds]
    for reach in sorted(set(bounds), reverse=True):
        lefts = [left for left in range(MAXDEG - 1) if bounds[left] == reach]
        levels(lefts[0], lefts[-1], reach)
    out_ref[...] = fields[0][pl.ds(RADIUS + home * cells, cells)]


def combine_kernel(count, weights_ref, *refs):
    panels, outs = refs[:count], refs[count:]
    for out, ref in enumerate(outs):
        total = None
        for index, panel in enumerate(panels):
            term = weights_ref[out, index : index + 1] * panel[...]
            total = term if total is None else total + term
        ref[...] = total


def in_vmem(x):
    return pltpu.with_memory_space_constraint(x, pltpu.VMEM)


def per_device(orbitals, potential, degree, owners, rotation):
    _, planes, cells, width = orbitals.shape
    n_orb = lax.axis_size("orb")
    me = lax.axis_index("orb")
    layout = Layout(lax.axis_size("dom"), cells, planes, width)
    vmem = pl.BlockSpec(memory_space=pltpu.VMEM)
    smem = pl.BlockSpec(memory_space=pltpu.SMEM)
    f32 = jnp.float32
    slab = pltpu.VMEM((cells, planes, width), f32)
    window = pltpu.VMEM((layout.window, planes, width), f32)
    padded = pltpu.VMEM((layout.window + 2 * RADIUS, planes, width), f32)

    orbital = jnp.transpose(orbitals[0], (1, 0, 2)).astype(f32)
    potential = jnp.transpose(potential, (1, 0, 2))
    half = lax.dynamic_slice_in_dim(potential, me % 2 * (cells // 2), cells // 2, 0)
    packed = jnp.concatenate([orbital, half], 0)
    arrived = [lax.ppermute(packed, "dom", p) for p in layout.pairs]
    coefficients = jnp.pad(rotation[:, 0, 0].astype(f32), (0, planes - STEPS))
    coefficients = jnp.broadcast_to(coefficients[None, :, None], (1, planes, width))
    halves = pl.pallas_call(
        functools.partial(halves_kernel, cells),
        out_shape=pltpu.VMEM((len(arrived) * (cells // 2) + 1, planes, width), f32),
        in_specs=[vmem] * (1 + len(arrived)),
        out_specs=vmem,
    )(*[in_vmem(x) for x in [coefficients] + arrived])
    swapped = lax.ppermute(halves, "orb", xor_pairs(n_orb, 1))

    matrices = [in_vmem(jnp.asarray(m)) for m in layout.matrices]
    operands = matrices + [in_vmem(x) for x in [packed] + arrived]
    start, taps = pl.pallas_call(
        functools.partial(open_kernel, layout),
        out_shape=(padded, window),
        in_specs=[vmem] * len(operands),
        out_specs=(vmem, vmem),
    )(*operands)
    operands = matrices + [in_vmem(x) for x in [potential, swapped, start, taps] + arrived]
    panel = pl.pallas_call(
        functools.partial(chain_kernel, layout),
        out_shape=slab,
        in_specs=[smem] + [vmem] * len(operands),
        out_specs=vmem,
        scratch_shapes=[padded, padded, window],
    )(degree, *operands)

    *near, last = sorted(range(2, n_orb, 2), key=lambda m: (m % 4 == 2, m))
    far = lax.ppermute(coefficients[0, :8], "orb", xor_pairs(n_orb, last))[:STEPS]

    def weights(columns, held):
        chosen = (owners[:, None] == jnp.stack([me ^ m for m in held])[None, :]).astype(f32)
        return jnp.sum(jnp.stack(columns)[:, :, None, :] * chosen[None, :, :, None], 1)

    def combined(columns, held, panels):
        return pl.pallas_call(
            functools.partial(combine_kernel, len(panels)),
            out_shape=(slab,) * len(columns),
            in_specs=[vmem] * (1 + len(panels)),
            out_specs=(vmem,) * len(columns),
        )(in_vmem(weights(columns, held)), *[in_vmem(p) for p in panels])

    panels = [panel] + [lax.ppermute(panel, "orb", xor_pairs(n_orb, m)) for m in near]
    beside = lax.ppermute(panel, "orb", xor_pairs(n_orb, 1))
    (sent,) = combined([far], [0, 1], [panel, beside])
    received = lax.ppermute(sent, "orb", xor_pairs(n_orb, last))
    mine, theirs = combined([coefficients[0, :STEPS], swapped[-1, :STEPS]], [0] + near, panels)
    rotated = mine + lax.ppermute(theirs, "orb", xor_pairs(n_orb, 1)) + received
    return tuple(jnp.transpose(x, (1, 0, 2))[None] for x in (panel, rotated))


def solution(mesh):
    placed = (
        P("orb", None, "dom", None),
        P(None, "dom", None),
        P("orb"),
        P(),
        P(None, None, "orb"),
    )
    return jax.shard_map(
        per_device,
        mesh=mesh,
        in_specs=placed,
        out_specs=(P("orb", None, "dom", None), P("orb", None, "dom", None)),
        check_vma=False,
    )
```

profile of v0, /device:TPU:0, one launch (start us, length us, event | category | flops | bytes accessed | tf_op | source)
XLA Modules:
  0.0 29.1 jit_solution(1620414551406654271)
XLA Ops:
  0.6 0.0 copy-start.3
  0.7 0.8 %convert_bitcast_fusion = f32[12,16,128]{2,1,0:T(8,128)S(1)} fusion(bf16[1,16,12,128]{3,1,2,0:T(8,128)(2,1)} %param.8), kind=kLoop, calls=%fused_computation.1 | loop fusion | flops 24576 | bytes 147456 | tf_op jit(solution)/shard_map/convert_element_type | solution.py:243
  1.5 0.0 copy-done.3
  1.5 0.0 copy-start.5
  1.5 3.0 %collective-permute-start = (f32[18,16,128]{2,1,0:T(8,128)S(1)}, f32[18,16,128]{2,1,0:T(8,128)S(1)}, u32[]{:S(2)}, u32[]{:S(2)}) collective-permute-start(f32[18,16,128]{2,1,0:T(8,128)S(1)} %pad_maximum_fusion.refs_3_), channel_id=1, source_target_pairs={{0,1},{1,0},{2,3},{3,2},{4,5},{5,4},{6,7},{7,6},{8,9},{9,8},{10,11... | collective-permute-start | bytes 442376 | tf_op jit(solution)/shard_map/ppermute | solution.py:247
  4.6 1.5 %collective-permute-start.1 = (f32[18,16,128]{2,1,0:T(8,128)S(1)}, f32[18,16,128]{2,1,0:T(8,128)S(1)}, u32[]{:S(2)}, u32[]{:S(2)}) collective-permute-start(f32[18,16,128]{2,1,0:T(8,128)S(1)} %pad_maximum_fusion.refs_3_), channel_id=1, source_target_pairs={{0,2},{1,3},{2,0},{3,1},{4,6},{5,7},{6,4},{7,5},{8,10},{9,11},{10,... | collective-permute-start | bytes 442376 | tf_op jit(solution)/shard_map/ppermute | solution.py:247
  6.1 0.0 collective-permute-start.2
  6.1 0.0 copy-done.5
  6.1 0.1 squeeze.2
  6.2 4.1 %collective-permute-start.7 = (f32[8,128]{1,0:T(8,128)S(1)}, f32[8,128]{1,0:T(8,128)S(1)}, u32[]{:S(2)}, u32[]{:S(2)}) collective-permute-start(f32[8,128]{1,0:T(8,128)S(1)} %squeeze.2), channel_id=1, source_target_pairs={{0,24},{4,28},{8,16},{12,20},{16,8},{20,12},{24,0},{28,4},{1,25},{... | collective-permute-start | bytes 12296 | tf_op jit(solution)/shard_map/ppermute | solution.py:276
  10.2 0.0 copy-start.4
  10.2 0.1 pad_add_fusion
  10.3 0.6 %copy-done.4 = s32[4]{0:T(128)S(1)} copy-done((s32[4]{0:T(128)S(1)}, s32[4]{0:T(128)}, u32[]{:S(2)}) %copy-start.4) | copy-done | bytes 40
  10.9 0.1 compare_convert_fusion.1
  11.0 0.1 pad_add_fusion.1
  11.0 0.0 collective-permute-done.refs_0_.refs_4_.refs_7_
  11.1 2.0 %collective-permute-done.1.refs_1_.refs_5_.refs_8_ = f32[18,16,128]{2,1,0:T(8,128)S(1)} collective-permute-done((f32[18,16,128]{2,1,0:T(8,128)S(1)}, f32[18,16,128]{2,1,0:T(8,128)S(1)}, u32[]{:S(2)}, u32[]{:S(2)}) %collective-permute-start.1) | collective-permute-done | bytes 147488 | tf_op jit(solution)/shard_map/ppermute | solution.py:247
  13.0 0.0 collective-permute-done.2.refs_2_.refs_6_.refs_9_
  13.0 0.1 broadcast_in_dim.8.coefficients_ref
  13.1 0.0 copy-start
  13.1 0.0 copy-start.1
  13.1 0.0 copy-start.2
  13.1 0.1 collective-permute-start.3
  13.2 0.1 compare_convert_fusion
  14.0 0.0 collective-permute-done.7
  14.0 0.1 multiply_reduce_fusion.1
  14.1 0.0 copy-done
  14.1 0.0 copy-done.1
  14.1 0.1 copy-done.2
  14.1 0.4 %shard_map.96 = (f32[60,16,128]{2,1,0:T(8,128)S(1)}, f32[48,16,128]{2,1,0:T(8,128)S(1)}) custom-call(bf16[256,256]{1,0:T(8,128)(2,1)S(1)} %copy-done, bf16[192,192]{1,0:T(8,128)(2,1)S(1)} %copy-done.2, bf16[256,256]{1,0:T(8,128)(2,1)S(1)} %copy-done.1, f32[18,16,128]{2,1,0:T(8,128)S(1)} %pad_maximum_fusion.refs_3_, ...), custom_call_target="tpu_custom_call" | custom-call | tf_op jit(solution)/shard_map/pallas_call | solution.py:260
  14.5 0.0 collective-permute-done.3.refs_4_
  14.6 2.0 %shard_map.97.refs_0_ = f32[12,16,128]{2,1,0:T(8,128)S(1)} custom-call(s32[1]{0:T(128)S(6)} %copy.11.degree_ref, bf16[256,256]{1,0:T(8,128)(2,1)S(1)} %copy-done, bf16[192,192]{1,0:T(8,128)(2,1)S(1)} %copy-done.2, bf16[256,256]{1,0:T(8,128)(2,1)S(1)} %copy-done.1, f32[12,16,128]{2,1,0:T(8,128)S(1)} %bitcast.24, ...), custom_call_target="tpu_custom_call" | custom-call | tf_op jit(solution)/shard_map/pallas_call | solution.py:267
  16.6 0.1 collective-permute-start.8
  16.7 1.4 %collective-permute-start.4 = (f32[12,16,128]{2,1,0:T(8,128)S(1)}, f32[12,16,128]{2,1,0:T(8,128)S(1)}, u32[]{:S(2)}, u32[]{:S(2)}) collective-permute-start(f32[12,16,128]{2,1,0:T(8,128)S(1)} %shard_map.97.refs_0_), channel_id=1, source_target_pairs={{0,16},{4,20},{8,24},{12,28},{16,0},{20,4},{24,8},{28,12},{1,17},{... | collective-permute-start | bytes 294920 | tf_op jit(solution)/shard_map/ppermute | solution.py:290
  18.0 3.1 %collective-permute-start.5 = (f32[12,16,128]{2,1,0:T(8,128)S(1)}, f32[12,16,128]{2,1,0:T(8,128)S(1)}, u32[]{:S(2)}, u32[]{:S(2)}) collective-permute-start(f32[12,16,128]{2,1,0:T(8,128)S(1)} %shard_map.97.refs_0_), channel_id=1, source_target_pairs={{0,8},{4,12},{8,0},{12,4},{16,24},{20,28},{24,16},{28,20},{1,9},{5... | collective-permute-start | bytes 294920 | tf_op jit(solution)/shard_map/ppermute | solution.py:290
  21.2 0.1 broadcast_in_dim.10
  21.3 0.1 multiply_reduce_fusion.weights_ref
  21.4 0.0 collective-permute-done.8.refs_1_
  21.4 0.5 %collective-permute-start.9 = (f32[12,16,128]{2,1,0:T(8,128)S(1)}, f32[12,16,128]{2,1,0:T(8,128)S(1)}, u32[]{:S(2)}, u32[]{:S(2)}) collective-permute-start(f32[12,16,128]{2,1,0:T(8,128)S(1)} %shard_map.99), channel_id=1, source_target_pairs={{0,24},{4,28},{8,16},{12,20},{16,8},{20,12},{24,0},{28,4},{1,25},{... | collective-permute-start | bytes 294920 | tf_op jit(solution)/shard_map/ppermute | solution.py:293
  21.9 3.4 %collective-permute-done.4.refs_1_ = f32[12,16,128]{2,1,0:T(8,128)S(1)} collective-permute-done((f32[12,16,128]{2,1,0:T(8,128)S(1)}, f32[12,16,128]{2,1,0:T(8,128)S(1)}, u32[]{:S(2)}, u32[]{:S(2)}) %collective-permute-start.4) | collective-permute-done | bytes 98336 | tf_op jit(solution)/shard_map/ppermute | solution.py:290
  25.4 0.0 collective-permute-done.5.refs_2_
  25.4 0.1 collective-permute-start.6
  25.5 0.6 %copy.10 = f32[1,16,12,128]{3,1,2,0:T(8,128)} copy(f32[1,16,12,128]{3,1,2,0:T(8,128)S(1)} %bitcast.23) | data formatting | bytes 196608
  26.1 2.3 %collective-permute-done.9 = f32[12,16,128]{2,1,0:T(8,128)S(1)} collective-permute-done((f32[12,16,128]{2,1,0:T(8,128)S(1)}, f32[12,16,128]{2,1,0:T(8,128)S(1)}, u32[]{:S(2)}, u32[]{:S(2)}) %collective-permute-start.9) | collective-permute-done | bytes 98336 | tf_op jit(solution)/shard_map/ppermute | solution.py:293
  28.4 0.0 collective-permute-done.6
  28.4 0.7 %add_bitcast_fusion = f32[1,16,12,128]{3,1,2,0:T(8,128)} fusion(f32[12,16,128]{2,1,0:T(8,128)S(1)} %collective-permute-done.9, f32[12,16,128]{2,1,0:T(8,128)S(1)} %get-tuple-element.8, f32[12,16,128]{2,1,0:T(8,128)S(1)} %collective-permute-done.6), kind=kLoop, calls=%fused_computation.2 | loop fusion | flops 49152 | bytes 393216 | tf_op jit(solution)/shard_map/broadcast_in_dim | solution.py:296
  (11 shorter events, 0.1 us)
Async XLA Ops:
  0.6 0.9 %copy-start.3 = (f32[16,12,128]{2,0,1:T(8,128)S(1)}, f32[16,12,128]{2,0,1:T(8,128)}, u32[]{:S(2)}) copy-start(f32[16,12,128]{2,0,1:T(8,128)} %param.9) | copy-start | bytes 294916
  1.5 4.6 %copy-start.5 = (bf16[4,1,1]{0,2,1:T(2,128)(2,1)S(1)}, bf16[4,1,1]{0,2,1:T(2,128)(2,1)}, u32[]{:S(2)}) copy-start(bf16[4,1,1]{0,2,1:T(2,128)(2,1)} %param.12) | copy-start | bytes 28
  1.5 9.5 %collective-permute-start = (f32[18,16,128]{2,1,0:T(8,128)S(1)}, f32[18,16,128]{2,1,0:T(8,128)S(1)}, u32[]{:S(2)}, u32[]{:S(2)}) collective-permute-start(f32[18,16,128]{2,1,0:T(8,128)S(1)} %pad_maximum_fusion.refs_3_), channel_id=1, source_target_pairs={{0,1},{1,0},{2,3},{3,2},{4,5},{5,4},{6,7},{7,6},{8,9},{9,8},{10,11... | collective-permute-start | bytes 442376 | tf_op jit(solution)/shard_map/ppermute | solution.py:247
  4.6 8.5 %collective-permute-start.1 = (f32[18,16,128]{2,1,0:T(8,128)S(1)}, f32[18,16,128]{2,1,0:T(8,128)S(1)}, u32[]{:S(2)}, u32[]{:S(2)}) collective-permute-start(f32[18,16,128]{2,1,0:T(8,128)S(1)} %pad_maximum_fusion.refs_3_), channel_id=1, source_target_pairs={{0,2},{1,3},{2,0},{3,1},{4,6},{5,7},{6,4},{7,5},{8,10},{9,11},{10,... | collective-permute-start | bytes 442376 | tf_op jit(solution)/shard_map/ppermute | solution.py:247
  6.1 7.0 %collective-permute-start.2 = (f32[18,16,128]{2,1,0:T(8,128)S(1)}, f32[18,16,128]{2,1,0:T(8,128)S(1)}, u32[]{:S(2)}, u32[]{:S(2)}) collective-permute-start(f32[18,16,128]{2,1,0:T(8,128)S(1)} %pad_maximum_fusion.refs_3_), channel_id=1, source_target_pairs={{0,3},{1,2},{2,1},{3,0},{4,7},{5,6},{6,5},{7,4},{8,11},{9,10},{10,... | collective-permute-start | bytes 442376 | tf_op jit(solution)/shard_map/ppermute | solution.py:247
  6.2 7.8 %collective-permute-start.7 = (f32[8,128]{1,0:T(8,128)S(1)}, f32[8,128]{1,0:T(8,128)S(1)}, u32[]{:S(2)}, u32[]{:S(2)}) collective-permute-start(f32[8,128]{1,0:T(8,128)S(1)} %squeeze.2), channel_id=1, source_target_pairs={{0,24},{4,28},{8,16},{12,20},{16,8},{20,12},{24,0},{28,4},{1,25},{... | collective-permute-start | bytes 12296 | tf_op jit(solution)/shard_map/ppermute | solution.py:276
  10.2 0.7 %copy-start.4 = (s32[4]{0:T(128)S(1)}, s32[4]{0:T(128)}, u32[]{:S(2)}) copy-start(s32[4]{0:T(128)} %param.11) | copy-start | bytes 52
  13.1 1.0 %copy-start = (bf16[256,256]{1,0:T(8,128)(2,1)S(1)}, bf16[256,256]{1,0:T(8,128)(2,1)}, u32[]{:S(2)}) copy-start(bf16[256,256]{1,0:T(8,128)(2,1)} %constant.36.clone.refs_0_) | copy-start | bytes 393220
  13.1 1.0 %copy-start.1 = (bf16[256,256]{1,0:T(8,128)(2,1)S(1)}, bf16[256,256]{1,0:T(8,128)(2,1)}, u32[]{:S(2)}) copy-start(bf16[256,256]{1,0:T(8,128)(2,1)} %constant.38.clone.refs_2_) | copy-start | bytes 393220
  13.1 1.0 %copy-start.2 = (bf16[192,192]{1,0:T(8,128)(2,1)S(1)}, bf16[192,192]{1,0:T(8,128)(2,1)}, u32[]{:S(2)}) copy-start(bf16[192,192]{1,0:T(8,128)(2,1)} %constant.37.clone.refs_1_) | copy-start | bytes 221188
  13.1 1.4 %collective-permute-start.3 = (f32[19,16,128]{2,1,0:T(8,128)S(1)}, f32[19,16,128]{2,1,0:T(8,128)S(1)}, u32[]{:S(2)}, u32[]{:S(2)}) collective-permute-start(f32[19,16,128]{2,1,0:T(8,128)S(1)} %shard_map.95), channel_id=1, source_target_pairs={{0,4},{4,0},{8,12},{12,8},{16,20},{20,16},{24,28},{28,24},{1,5},{5... | collective-permute-start | bytes 466952 | tf_op jit(solution)/shard_map/ppermute | solution.py:256
  16.6 4.8 %collective-permute-start.8 = (f32[12,16,128]{2,1,0:T(8,128)S(1)}, f32[12,16,128]{2,1,0:T(8,128)S(1)}, u32[]{:S(2)}, u32[]{:S(2)}) collective-permute-start(f32[12,16,128]{2,1,0:T(8,128)S(1)} %shard_map.97.refs_0_), channel_id=1, source_target_pairs={{0,4},{4,0},{8,12},{12,8},{16,20},{20,16},{24,28},{28,24},{1,5},{5... | collective-permute-start | bytes 294920 | tf_op jit(solution)/shard_map/ppermute | solution.py:291
  16.7 8.7 %collective-permute-start.4 = (f32[12,16,128]{2,1,0:T(8,128)S(1)}, f32[12,16,128]{2,1,0:T(8,128)S(1)}, u32[]{:S(2)}, u32[]{:S(2)}) collective-permute-start(f32[12,16,128]{2,1,0:T(8,128)S(1)} %shard_map.97.refs_0_), channel_id=1, source_target_pairs={{0,16},{4,20},{8,24},{12,28},{16,0},{20,4},{24,8},{28,12},{1,17},{... | collective-permute-start | bytes 294920 | tf_op jit(solution)/shard_map/ppermute | solution.py:290
  18.0 7.3 %collective-permute-start.5 = (f32[12,16,128]{2,1,0:T(8,128)S(1)}, f32[12,16,128]{2,1,0:T(8,128)S(1)}, u32[]{:S(2)}, u32[]{:S(2)}) collective-permute-start(f32[12,16,128]{2,1,0:T(8,128)S(1)} %shard_map.97.refs_0_), channel_id=1, source_target_pairs={{0,8},{4,12},{8,0},{12,4},{16,24},{20,28},{24,16},{28,20},{1,9},{5... | collective-permute-start | bytes 294920 | tf_op jit(solution)/shard_map/ppermute | solution.py:290
  21.4 7.0 %collective-permute-start.9 = (f32[12,16,128]{2,1,0:T(8,128)S(1)}, f32[12,16,128]{2,1,0:T(8,128)S(1)}, u32[]{:S(2)}, u32[]{:S(2)}) collective-permute-start(f32[12,16,128]{2,1,0:T(8,128)S(1)} %shard_map.99), channel_id=1, source_target_pairs={{0,24},{4,28},{8,16},{12,20},{16,8},{20,12},{24,0},{28,4},{1,25},{... | collective-permute-start | bytes 294920 | tf_op jit(solution)/shard_map/ppermute | solution.py:293
  25.4 3.0 %collective-permute-start.6 = (f32[12,16,128]{2,1,0:T(8,128)S(1)}, f32[12,16,128]{2,1,0:T(8,128)S(1)}, u32[]{:S(2)}, u32[]{:S(2)}) collective-permute-start(f32[12,16,128]{2,1,0:T(8,128)S(1)} %get-tuple-element.9), channel_id=1, source_target_pairs={{0,4},{4,0},{8,12},{12,8},{16,20},{20,16},{24,28},{28,24},{1,5},{5... | collective-permute-start | bytes 294920 | tf_op jit(solution)/shard_map/ppermute | solution.py:295
where the time goes:
time: 29.2 us; the launch traced here: 29.1 us
  starting transfers between devices  13.9 us (48%)
  waiting for transfers between devices  7.73 us (26%)
  Pallas kernels  2.51 us (9%)
  other arithmetic  1.99 us (7%)
  local copies, waits for them, and re-layouts  1.55 us (5%)
  between operations  1.44 us (5%)
    ppermute x3, starting transfers between devices, per_device(): arrived = [lax.ppermute(packed, 'dom', p) for p in layout.pairs]  4.54 us
    ppermute x2, starting transfers between devices, per_device(): lax.ppermute(panel, 'orb', xor_pairs(n_orb, m))  4.5 us
    ppermute x1, starting transfers between devices, per_device(): lax.ppermute(coefficients[0, :8], 'orb', xor_pairs(n_orb, last))[:STEPS]  4.06 us
    ppermute x2, waiting for transfers between devices, per_device(): lax.ppermute(panel, 'orb', xor_pairs(n_orb, m))  3.43 us
    ppermute x1, waiting for transfers between devices, per_device(): received = lax.ppermute(sent, 'orb', xor_pairs(n_orb, last))  2.29 us
    pallas_call x1, Pallas kernels, per_device(): pl.pallas_call(functools.partial(chain_kernel, layout), out_shape=slab, i...  2.04 us
    ppermute x3, waiting for transfers between devices, per_device(): arrived = [lax.ppermute(packed, 'dom', p) for p in layout.pairs]  1.98 us
    unnamed x13, local copies, waits for them, and re-layouts  1.32 us
  transfers between devices with their start and end apart: 10, of which 3 were waited for; matrix products, arithmetic and copies ran while one was open for 5% of the time, Pallas kernels for 2%

commit v1 on v0

--- a/solution.py
+++ b/solution.py
@@ -61,7 +61,7 @@
         halo = -(-RADIUS * MAXDEG // cells)
         self.whole = n_dom <= 2 * halo + 1
         if self.whole:
-            self.slots = list(range(1, n_dom))
+            self.slots = list(range(n_dom - 1, 0, -1))
             self.pairs = [xor_pairs(n_dom, k) for k in self.slots]
             self.window = n_dom * cells
             extents = {min(cells + 2 * RADIUS * left, self.window) for left in range(MAXDEG)}
@@ -121,6 +121,13 @@
             target[spot] = target[spot] + plane_sum.reshape(group, planes, width)
 
 
+def early_kernel(*refs):
+    count = len(refs) // 2
+    refs[count][0] = refs[0][0]
+    for source, target in zip(refs[1:count], refs[count + 1 :]):
+        target[...] = source[...]
+
+
 def halves_kernel(cells, coefficients_ref, *refs):
     *blocks, out_ref = refs
     half = cells // 2
@@ -245,7 +252,17 @@
     half = lax.dynamic_slice_in_dim(potential, me % 2 * (cells // 2), cells // 2, 0)
     packed = jnp.concatenate([orbital, half], 0)
     arrived = [lax.ppermute(packed, "dom", p) for p in layout.pairs]
-    coefficients = jnp.pad(rotation[:, 0, 0].astype(f32), (0, planes - STEPS))
+    matrices = [in_vmem(jnp.asarray(m)) for m in layout.matrices]
+    column = rotation[:, 0, 0].astype(f32)
+    early = pl.pallas_call(
+        early_kernel,
+        out_shape=[pltpu.SMEM((1,), jnp.int32)] + [pltpu.VMEM(m.shape, m.dtype) for m in layout.matrices],
+        in_specs=[smem] + [vmem] * len(matrices),
+        out_specs=[smem] + [vmem] * len(matrices),
+    )(degree, *matrices)
+    column, degree, *matrices = lax.optimization_barrier((column, *early))
+    matrices = [in_vmem(m) for m in matrices]
+    coefficients = jnp.pad(column, (0, planes - STEPS))
     coefficients = jnp.broadcast_to(coefficients[None, :, None], (1, planes, width))
     halves = pl.pallas_call(
         functools.partial(halves_kernel, cells),
@@ -255,7 +272,6 @@
     )(*[in_vmem(x) for x in [coefficients] + arrived])
     swapped = lax.ppermute(halves, "orb", xor_pairs(n_orb, 1))
 
-    matrices = [in_vmem(jnp.asarray(m)) for m in layout.matrices]
     operands = matrices + [in_vmem(x) for x in [packed] + arrived]
     start, taps = pl.pallas_call(
         functools.partial(open_kernel, layout),
@@ -270,7 +286,7 @@
         in_specs=[smem] + [vmem] * len(operands),
         out_specs=vmem,
         scratch_shapes=[padded, padded, window],
-    )(degree, *operands)
+    )(pltpu.with_memory_space_constraint(degree, pltpu.SMEM), *operands)
 
     *near, last = sorted(range(2, n_orb, 2), key=lambda m: (m % 4 == 2, m))
     far = lax.ppermute(coefficients[0, :8], "orb", xor_pairs(n_orb, last))[:STEPS]

time: 29.2 us -> 29.6 us (1.014); the launches traced: 29.1 us -> 30.1 us
  waiting for transfers between devices: 7.73 us -> 9.34 us
  Pallas kernels: 2.51 us -> 1.52 us
  starting transfers between devices: 13.9 us -> 14.3 us
    ppermute x2, waiting for transfers between devices: 3.43 us -> 6.88 us  [per_device(): lax.ppermute(panel, 'orb', xor_pairs(n_orb, m))]
    ppermute x1, waiting for transfers between devices: 2.29 us -> 0.01 us  [per_device(): received = lax.ppermute(sent, 'orb', xor_pairs(n_orb, last))]
    pallas_call x1, Pallas kernels: 2.04 us -> 1.02 us  [per_device(): pl.pallas_call(functools.partial(chain_kernel, layout), out_shape=slab, i...]
    ppermute x3, waiting for transfers between devices: 1.98 us -> 1.03 us  [per_device(): arrived = [lax.ppermute(packed, 'dom', p) for p in layout.pairs]]
    ppermute x2, starting transfers between devices: 4.5 us -> 3.57 us  [per_device(): lax.ppermute(panel, 'orb', xor_pairs(n_orb, m))]
    ppermute x1, waiting for transfers between devices: 0.03 us -> 0.79 us  [per_device(): swapped = lax.ppermute(halves, 'orb', xor_pairs(n_orb, 1))]
    ppermute x1, starting transfers between devices: 0.07 us -> 0.81 us  [per_device(): beside = lax.ppermute(panel, 'orb', xor_pairs(n_orb, 1))]
    ppermute x1, waiting for transfers between devices: 0.01 us -> 0.64 us  [per_device(): rotated = mine + lax.ppermute(theirs, 'orb', xor_pairs(n_orb, 1)) + received]
  transfers between devices with their start and end apart: 10 -> 10, of which waited for: 3 -> 6; matrix products, arithmetic and copies ran while one was open for 5% -> 4% of each run, Pallas kernels for 2% -> 2%
where the time goes in v1:
time: 29.6 us; the launch traced here: 30.1 us
  starting transfers between devices  14.3 us (48%)
  waiting for transfers between devices  9.34 us (32%)
  other arithmetic  1.99 us (7%)
  Pallas kernels  1.52 us (5%)
  local copies, waits for them, and re-layouts  1.5 us (5%)
  between operations  1.45 us (5%)
    ppermute x2, waiting for transfers between devices, per_device(): lax.ppermute(panel, 'orb', xor_pairs(n_orb, m))  6.88 us
    ppermute x3, starting transfers between devices, per_device(): arrived = [lax.ppermute(packed, 'dom', p) for p in layout.pairs]  4.6 us
    ppermute x1, starting transfers between devices, per_device(): lax.ppermute(coefficients[0, :8], 'orb', xor_pairs(n_orb, last))[:STEPS]  4.01 us
    ppermute x2, starting transfers between devices, per_device(): lax.ppermute(panel, 'orb', xor_pairs(n_orb, m))  3.57 us
    unnamed x13, local copies, waits for them, and re-layouts  1.28 us
    ppermute x1, starting transfers between devices, per_device(): received = lax.ppermute(sent, 'orb', xor_pairs(n_orb, last))  1.16 us
    ppermute x3, waiting for transfers between devices, per_device(): arrived = [lax.ppermute(packed, 'dom', p) for p in layout.pairs]  1.03 us
    pallas_call x1, Pallas kernels, per_device(): pl.pallas_call(functools.partial(chain_kernel, layout), out_shape=slab, i...  1.02 us
  transfers between devices with their start and end apart: 10, of which 6 were waited for; matrix products, arithmetic and copies ran while one was open for 4% of the time, Pallas kernels for 2%

profile of v1, /device:TPU:0, one launch (start us, length us, event | category | flops | bytes accessed | tf_op | source)
XLA Modules:
  0.0 30.1 jit_solution(5013987378281653643)
XLA Ops:
  0.6 0.0 copy-start
  0.7 0.8 %convert_bitcast_fusion = f32[12,16,128]{2,1,0:T(8,128)S(1)} fusion(bf16[1,16,12,128]{3,1,2,0:T(8,128)(2,1)} %param.8), kind=kLoop, calls=%fused_computation.1 | loop fusion | flops 24576 | bytes 147456 | tf_op jit(solution)/shard_map/convert_element_type | solution.py:250
  1.5 0.0 copy-done
  1.5 0.0 copy-start.3
  1.5 0.0 copy-start.5
  1.5 0.0 copy-start.1
  1.6 0.0 copy-start.2
  1.6 4.0 %collective-permute-start = (f32[18,16,128]{2,1,0:T(8,128)S(1)}, f32[18,16,128]{2,1,0:T(8,128)S(1)}, u32[]{:S(2)}, u32[]{:S(2)}) collective-permute-start(f32[18,16,128]{2,1,0:T(8,128)S(1)} %pad_maximum_fusion.refs_3_), channel_id=1, source_target_pairs={{0,3},{1,2},{2,1},{3,0},{4,7},{5,6},{6,5},{7,4},{8,11},{9,10},{10,... | collective-permute-start | bytes 442376 | tf_op jit(solution)/shard_map/ppermute | solution.py:254
  5.5 0.5 %collective-permute-start.1 = (f32[18,16,128]{2,1,0:T(8,128)S(1)}, f32[18,16,128]{2,1,0:T(8,128)S(1)}, u32[]{:S(2)}, u32[]{:S(2)}) collective-permute-start(f32[18,16,128]{2,1,0:T(8,128)S(1)} %pad_maximum_fusion.refs_3_), channel_id=1, source_target_pairs={{0,2},{1,3},{2,0},{3,1},{4,6},{5,7},{6,4},{7,5},{8,10},{9,11},{10,... | collective-permute-start | bytes 442376 | tf_op jit(solution)/shard_map/ppermute | solution.py:254
  6.1 0.1 collective-permute-start.2
  6.2 0.0 copy-done.5
  6.8 0.0 copy-done.3
  6.9 0.0 copy-done.1
  6.9 0.0 copy-done.2
  6.9 0.1 squeeze.2
  7.0 4.0 %collective-permute-start.7 = (f32[8,128]{1,0:T(8,128)S(1)}, f32[8,128]{1,0:T(8,128)S(1)}, u32[]{:S(2)}, u32[]{:S(2)}) collective-permute-start(f32[8,128]{1,0:T(8,128)S(1)} %squeeze.2), channel_id=1, source_target_pairs={{0,24},{4,28},{8,16},{12,20},{16,8},{20,12},{24,0},{28,4},{1,25},{... | collective-permute-start | bytes 12296 | tf_op jit(solution)/shard_map/ppermute | solution.py:292
  11.0 0.0 copy-start.4
  11.0 0.1 pad_add_fusion
  11.1 0.6 %copy-done.4 = s32[4]{0:T(128)S(1)} copy-done((s32[4]{0:T(128)S(1)}, s32[4]{0:T(128)}, u32[]{:S(2)}) %copy-start.4) | copy-done | bytes 40
  11.7 0.1 compare_convert_fusion.1
  11.7 0.1 pad_add_fusion.1
  11.8 0.0 collective-permute-done.refs_0_.refs_4_.refs_7_
  11.8 0.7 %collective-permute-done.1.refs_1_.refs_5_.refs_8_ = f32[18,16,128]{2,1,0:T(8,128)S(1)} collective-permute-done((f32[18,16,128]{2,1,0:T(8,128)S(1)}, f32[18,16,128]{2,1,0:T(8,128)S(1)}, u32[]{:S(2)}, u32[]{:S(2)}) %collective-permute-start.1) | collective-permute-done | bytes 147488 | tf_op jit(solution)/shard_map/ppermute | solution.py:254
  12.6 0.3 collective-permute-done.2.refs_2_.refs_6_.refs_9_
  12.8 0.1 broadcast_in_dim.8.coefficients_ref
  12.9 0.1 collective-permute-start.3
  13.0 0.1 compare_convert_fusion
  13.1 0.0 collective-permute-done.7
  13.1 0.1 multiply_reduce_fusion.1
  13.2 0.4 %shard_map.97 = (f32[60,16,128]{2,1,0:T(8,128)S(1)}, f32[48,16,128]{2,1,0:T(8,128)S(1)}) custom-call(bf16[256,256]{1,0:T(8,128)(2,1)S(1)} %get-tuple-element.20.refs_0_, bf16[192,192]{1,0:T(8,128)(2,1)S(1)} %get-tuple-element.21.refs_1_, bf16[256,256]{1,0:T(8,128)(2,1)S(1)} %get-tuple-element.22.refs_2_, f32[18,16,128]{2,1,0:T(8,128)S(1)} %pad_maximum_fusion.refs_3_, ...), custom_call_target="tpu_custom_call" | custom-call | tf_op jit(solution)/shard_map/pallas_call | solution.py:276
  13.6 0.8 %collective-permute-done.3.refs_4_ = f32[19,16,128]{2,1,0:T(8,128)S(1)} collective-permute-done((f32[19,16,128]{2,1,0:T(8,128)S(1)}, f32[19,16,128]{2,1,0:T(8,128)S(1)}, u32[]{:S(2)}, u32[]{:S(2)}) %collective-permute-start.3) | collective-permute-done | bytes 155680 | tf_op jit(solution)/shard_map/ppermute | solution.py:273
  14.4 1.0 %shard_map.98.refs_0_ = f32[12,16,128]{2,1,0:T(8,128)S(1)} custom-call(s32[1]{0:T(128)S(4)} %get-tuple-element.19.degree_ref, bf16[256,256]{1,0:T(8,128)(2,1)S(1)} %get-tuple-element.20.refs_0_, bf16[192,192]{1,0:T(8,128)(2,1)S(1)} %get-tuple-element.21.refs_1_, bf16[256,256]{1,0:T(8,128)(2,1)S(1)} %get-tuple-element.22.refs_2_, ...), custom_call_target="tpu_custom_call" | custom-call | tf_op jit(solution)/shard_map/pallas_call | solution.py:283
  15.4 0.8 %collective-permute-start.8 = (f32[12,16,128]{2,1,0:T(8,128)S(1)}, f32[12,16,128]{2,1,0:T(8,128)S(1)}, u32[]{:S(2)}, u32[]{:S(2)}) collective-permute-start(f32[12,16,128]{2,1,0:T(8,128)S(1)} %shard_map.98.refs_0_), channel_id=1, source_target_pairs={{0,4},{4,0},{8,12},{12,8},{16,20},{20,16},{24,28},{28,24},{1,5},{5... | collective-permute-start | bytes 294920 | tf_op jit(solution)/shard_map/ppermute | solution.py:307
  16.2 3.2 %collective-permute-start.4 = (f32[12,16,128]{2,1,0:T(8,128)S(1)}, f32[12,16,128]{2,1,0:T(8,128)S(1)}, u32[]{:S(2)}, u32[]{:S(2)}) collective-permute-start(f32[12,16,128]{2,1,0:T(8,128)S(1)} %shard_map.98.refs_0_), channel_id=1, source_target_pairs={{0,16},{4,20},{8,24},{12,28},{16,0},{20,4},{24,8},{28,12},{1,17},{... | collective-permute-start | bytes 294920 | tf_op jit(solution)/shard_map/ppermute | solution.py:306
  19.4 0.4 %collective-permute-start.5 = (f32[12,16,128]{2,1,0:T(8,128)S(1)}, f32[12,16,128]{2,1,0:T(8,128)S(1)}, u32[]{:S(2)}, u32[]{:S(2)}) collective-permute-start(f32[12,16,128]{2,1,0:T(8,128)S(1)} %shard_map.98.refs_0_), channel_id=1, source_target_pairs={{0,8},{4,12},{8,0},{12,4},{16,24},{20,28},{24,16},{28,20},{1,9},{5... | collective-permute-start | bytes 294920 | tf_op jit(solution)/shard_map/ppermute | solution.py:306
  19.8 0.1 broadcast_in_dim.10
  19.9 0.1 multiply_reduce_fusion.weights_ref
  19.9 0.0 collective-permute-done.8.refs_1_
  20.0 1.2 %collective-permute-start.9 = (f32[12,16,128]{2,1,0:T(8,128)S(1)}, f32[12,16,128]{2,1,0:T(8,128)S(1)}, u32[]{:S(2)}, u32[]{:S(2)}) collective-permute-start(f32[12,16,128]{2,1,0:T(8,128)S(1)} %shard_map.100), channel_id=1, source_target_pairs={{0,24},{4,28},{8,16},{12,20},{16,8},{20,12},{24,0},{28,4},{1,25},{... | collective-permute-start | bytes 294920 | tf_op jit(solution)/shard_map/ppermute | solution.py:309
  21.1 3.7 %collective-permute-done.4.refs_1_ = f32[12,16,128]{2,1,0:T(8,128)S(1)} collective-permute-done((f32[12,16,128]{2,1,0:T(8,128)S(1)}, f32[12,16,128]{2,1,0:T(8,128)S(1)}, u32[]{:S(2)}, u32[]{:S(2)}) %collective-permute-start.4) | collective-permute-done | bytes 98336 | tf_op jit(solution)/shard_map/ppermute | solution.py:306
  24.8 3.2 %collective-permute-done.5.refs_2_ = f32[12,16,128]{2,1,0:T(8,128)S(1)} collective-permute-done((f32[12,16,128]{2,1,0:T(8,128)S(1)}, f32[12,16,128]{2,1,0:T(8,128)S(1)}, u32[]{:S(2)}, u32[]{:S(2)}) %collective-permute-start.5) | collective-permute-done | bytes 98336 | tf_op jit(solution)/shard_map/ppermute | solution.py:306
  28.1 0.1 collective-permute-start.6
  28.1 0.6 %copy.10 = f32[1,16,12,128]{3,1,2,0:T(8,128)} copy(f32[1,16,12,128]{3,1,2,0:T(8,128)S(1)} %bitcast.23) | data formatting | bytes 196608
  28.8 0.0 collective-permute-done.9
  28.8 0.6 %collective-permute-done.6 = f32[12,16,128]{2,1,0:T(8,128)S(1)} collective-permute-done((f32[12,16,128]{2,1,0:T(8,128)S(1)}, f32[12,16,128]{2,1,0:T(8,128)S(1)}, u32[]{:S(2)}, u32[]{:S(2)}) %collective-permute-start.6) | collective-permute-done | bytes 98336 | tf_op jit(solution)/shard_map/ppermute | solution.py:311
  29.4 0.7 %add_bitcast_fusion = f32[1,16,12,128]{3,1,2,0:T(8,128)} fusion(f32[12,16,128]{2,1,0:T(8,128)S(1)} %collective-permute-done.9, f32[12,16,128]{2,1,0:T(8,128)S(1)} %get-tuple-element.26, f32[12,16,128]{2,1,0:T(8,128)S(1)} %collective-permute-done.6), kind=kLoop, calls=%fused_computation.2 | loop fusion | flops 49152 | bytes 393216 | tf_op jit(solution)/shard_map/broadcast_in_dim | solution.py:312
  (12 shorter events, 0.1 us)
Async XLA Ops:
  0.6 0.9 %copy-start = (f32[16,12,128]{2,0,1:T(8,128)S(1)}, f32[16,12,128]{2,0,1:T(8,128)}, u32[]{:S(2)}) copy-start(f32[16,12,128]{2,0,1:T(8,128)} %param.9) | copy-start | bytes 294916
  1.5 5.3 %copy-start.3 = (bf16[192,192]{1,0:T(8,128)(2,1)S(1)}, bf16[192,192]{1,0:T(8,128)(2,1)}, u32[]{:S(2)}) copy-start(bf16[192,192]{1,0:T(8,128)(2,1)} %constant.37.clone.refs_2_) | copy-start | bytes 221188
  1.5 4.7 %copy-start.5 = (bf16[4,1,1]{0,2,1:T(2,128)(2,1)S(1)}, bf16[4,1,1]{0,2,1:T(2,128)(2,1)}, u32[]{:S(2)}) copy-start(bf16[4,1,1]{0,2,1:T(2,128)(2,1)} %param.12) | copy-start | bytes 28
  1.5 5.3 %copy-start.1 = (bf16[256,256]{1,0:T(8,128)(2,1)S(1)}, bf16[256,256]{1,0:T(8,128)(2,1)}, u32[]{:S(2)}) copy-start(bf16[256,256]{1,0:T(8,128)(2,1)} %constant.36.clone.refs_1_) | copy-start | bytes 393220
  1.6 5.3 %copy-start.2 = (bf16[256,256]{1,0:T(8,128)(2,1)S(1)}, bf16[256,256]{1,0:T(8,128)(2,1)}, u32[]{:S(2)}) copy-start(bf16[256,256]{1,0:T(8,128)(2,1)} %constant.38.clone.refs_3_) | copy-start | bytes 393220
  1.6 10.2 %collective-permute-start = (f32[18,16,128]{2,1,0:T(8,128)S(1)}, f32[18,16,128]{2,1,0:T(8,128)S(1)}, u32[]{:S(2)}, u32[]{:S(2)}) collective-permute-start(f32[18,16,128]{2,1,0:T(8,128)S(1)} %pad_maximum_fusion.refs_3_), channel_id=1, source_target_pairs={{0,3},{1,2},{2,1},{3,0},{4,7},{5,6},{6,5},{7,4},{8,11},{9,10},{10,... | collective-permute-start | bytes 442376 | tf_op jit(solution)/shard_map/ppermute | solution.py:254
  5.5 7.0 %collective-permute-start.1 = (f32[18,16,128]{2,1,0:T(8,128)S(1)}, f32[18,16,128]{2,1,0:T(8,128)S(1)}, u32[]{:S(2)}, u32[]{:S(2)}) collective-permute-start(f32[18,16,128]{2,1,0:T(8,128)S(1)} %pad_maximum_fusion.refs_3_), channel_id=1, source_target_pairs={{0,2},{1,3},{2,0},{3,1},{4,6},{5,7},{6,4},{7,5},{8,10},{9,11},{10,... | collective-permute-start | bytes 442376 | tf_op jit(solution)/shard_map/ppermute | solution.py:254
  6.1 6.8 %collective-permute-start.2 = (f32[18,16,128]{2,1,0:T(8,128)S(1)}, f32[18,16,128]{2,1,0:T(8,128)S(1)}, u32[]{:S(2)}, u32[]{:S(2)}) collective-permute-start(f32[18,16,128]{2,1,0:T(8,128)S(1)} %pad_maximum_fusion.refs_3_), channel_id=1, source_target_pairs={{0,1},{1,0},{2,3},{3,2},{4,5},{5,4},{6,7},{7,6},{8,9},{9,8},{10,11... | collective-permute-start | bytes 442376 | tf_op jit(solution)/shard_map/ppermute | solution.py:254
  7.0 6.1 %collective-permute-start.7 = (f32[8,128]{1,0:T(8,128)S(1)}, f32[8,128]{1,0:T(8,128)S(1)}, u32[]{:S(2)}, u32[]{:S(2)}) collective-permute-start(f32[8,128]{1,0:T(8,128)S(1)} %squeeze.2), channel_id=1, source_target_pairs={{0,24},{4,28},{8,16},{12,20},{16,8},{20,12},{24,0},{28,4},{1,25},{... | collective-permute-start | bytes 12296 | tf_op jit(solution)/shard_map/ppermute | solution.py:292
  11.0 0.7 %copy-start.4 = (s32[4]{0:T(128)S(1)}, s32[4]{0:T(128)}, u32[]{:S(2)}) copy-start(s32[4]{0:T(128)} %param.11) | copy-start | bytes 52
  12.9 1.4 %collective-permute-start.3 = (f32[19,16,128]{2,1,0:T(8,128)S(1)}, f32[19,16,128]{2,1,0:T(8,128)S(1)}, u32[]{:S(2)}, u32[]{:S(2)}) collective-permute-start(f32[19,16,128]{2,1,0:T(8,128)S(1)} %shard_map.96), channel_id=1, source_target_pairs={{0,4},{4,0},{8,12},{12,8},{16,20},{20,16},{24,28},{28,24},{1,5},{5... | collective-permute-start | bytes 466952 | tf_op jit(solution)/shard_map/ppermute | solution.py:273
  15.4 4.5 %collective-permute-start.8 = (f32[12,16,128]{2,1,0:T(8,128)S(1)}, f32[12,16,128]{2,1,0:T(8,128)S(1)}, u32[]{:S(2)}, u32[]{:S(2)}) collective-permute-start(f32[12,16,128]{2,1,0:T(8,128)S(1)} %shard_map.98.refs_0_), channel_id=1, source_target_pairs={{0,4},{4,0},{8,12},{12,8},{16,20},{20,16},{24,28},{28,24},{1,5},{5... | collective-permute-start | bytes 294920 | tf_op jit(solution)/shard_map/ppermute | solution.py:307
  16.2 8.6 %collective-permute-start.4 = (f32[12,16,128]{2,1,0:T(8,128)S(1)}, f32[12,16,128]{2,1,0:T(8,128)S(1)}, u32[]{:S(2)}, u32[]{:S(2)}) collective-permute-start(f32[12,16,128]{2,1,0:T(8,128)S(1)} %shard_map.98.refs_0_), channel_id=1, source_target_pairs={{0,16},{4,20},{8,24},{12,28},{16,0},{20,4},{24,8},{28,12},{1,17},{... | collective-permute-start | bytes 294920 | tf_op jit(solution)/shard_map/ppermute | solution.py:306
  19.4 8.6 %collective-permute-start.5 = (f32[12,16,128]{2,1,0:T(8,128)S(1)}, f32[12,16,128]{2,1,0:T(8,128)S(1)}, u32[]{:S(2)}, u32[]{:S(2)}) collective-permute-start(f32[12,16,128]{2,1,0:T(8,128)S(1)} %shard_map.98.refs_0_), channel_id=1, source_target_pairs={{0,8},{4,12},{8,0},{12,4},{16,24},{20,28},{24,16},{28,20},{1,9},{5... | collective-permute-start | bytes 294920 | tf_op jit(solution)/shard_map/ppermute | solution.py:306
  20.0 8.8 %collective-permute-start.9 = (f32[12,16,128]{2,1,0:T(8,128)S(1)}, f32[12,16,128]{2,1,0:T(8,128)S(1)}, u32[]{:S(2)}, u32[]{:S(2)}) collective-permute-start(f32[12,16,128]{2,1,0:T(8,128)S(1)} %shard_map.100), channel_id=1, source_target_pairs={{0,24},{4,28},{8,16},{12,20},{16,8},{20,12},{24,0},{28,4},{1,25},{... | collective-permute-start | bytes 294920 | tf_op jit(solution)/shard_map/ppermute | solution.py:309
  28.1 1.4 %collective-permute-start.6 = (f32[12,16,128]{2,1,0:T(8,128)S(1)}, f32[12,16,128]{2,1,0:T(8,128)S(1)}, u32[]{:S(2)}, u32[]{:S(2)}) collective-permute-start(f32[12,16,128]{2,1,0:T(8,128)S(1)} %get-tuple-element.27), channel_id=1, source_target_pairs={{0,4},{4,0},{8,12},{12,8},{16,20},{20,16},{24,28},{28,24},{1,5},{5... | collective-permute-start | bytes 294920 | tf_op jit(solution)/shard_map/ppermute | solution.py:311
